TPU v7x, 32 devices: a whole 2x2x4 slice. The times are simulated.
32 devices in a mesh: section: 2 (over core), group: 2 (over y), shard: 8 (over z, x).
Axes of the slice: x: 2, y: 2, z: 4, core: 2. Of those that a mesh axis runs over, the one named last changes fastest.
Arguments:
- cache: bfloat16 [2, 2, 8, 8, 128, 2048], P('section', 'group', None, 'shard'), may hold values from -4 to 4
- queries: bfloat16 [2, 2, 8, 4, 16384], P('section', 'group', None, None, 'shard'), may hold values from -19 to 19
- fresh_kv: bfloat16 [2, 2, 8, 4, 2048], P('section', 'group', None, None, 'shard'), may hold values from -4 to 4
- lengths: int32 [2, 2, 8], P('section', 'group'), may hold values from 2 to 1020, as said below
- targets: int32 [2, 8], P('group'), may hold values from 0 to 2, as said below
Outputs:
- attended: bfloat16 [2, 2, 8, 4, 16384], P('section', 'group', None, None, 'shard')
- handed: bfloat16 [2, 2, 2, 2, 8, 128, 2048], P('section', 'group', None, None, 'shard')
Inputs may be any that keep to these rules, and one draw needn't show every extreme that they name: `lengths`: each row has at least two cached positions, and in every section and group some row has exactly 1020. `targets`: the value 2 means that the prompt is not handed this round; at most 2 rows of one prefill group name one decode group, and some decode group is named by exactly 2 rows of every prefill group.
All inputs are finite; a program needn't handle non-finite values.
Results may differ from a plain program's by a relative error of at most 0.0044.
Values may be sent and summed in bfloat16 or wider, within the bound.
A program may use at most 128 MiB of HBM per device.

v0:
```python
import math

import jax
import jax.numpy as jnp
from jax import lax
from jax.sharding import PartitionSpec as P

HQ = 128
KVH = 8
DH = 128
CAP = 2


NEGATIVE = -jnp.inf


def passed_along(block, axis, distance):
    devices = range(lax.axis_size(axis))
    route = [(i - distance, i) for i in devices if i - distance in devices]
    return lax.ppermute(block, axis, route)


def restripe(released):
    group_count, capacity, slot_count, kv_width = released.shape
    shard_count = lax.axis_size("shard")
    per_peer = slot_count // shard_count
    pieces = released.reshape(group_count, capacity, per_peer, shard_count, kv_width)
    ordered = jnp.transpose(pieces, (0, 3, 1, 2, 4)).reshape(
        group_count * shard_count, capacity, per_peer, kv_width
    )
    arrived = lax.all_to_all(ordered, ("group", "shard"), split_axis=0, concat_axis=0, tiled=True)
    arrived = arrived.reshape(group_count, shard_count, capacity, per_peer, kv_width)
    arrived = jnp.transpose(arrived, (0, 2, 1, 3, 4))
    return arrived.reshape(group_count, capacity, slot_count, kv_width)


def on_device(cache, queries, fresh_kv, lengths, targets):
    row_count = cache.shape[2]
    slot_count = cache.shape[4]
    kv_width = cache.shape[5]
    shard_count = lax.axis_size("shard")
    group_count = lax.axis_size("group")
    section_id = lax.axis_index("section")
    shard_id = lax.axis_index("shard")
    group_size = HQ // KVH
    key_width = KVH * DH
    score_scale = 1.0 / math.sqrt(DH)
    all_queries, all_fresh = (
        lax.all_gather(queries, "shard", axis=4, tiled=True),
        lax.all_gather(fresh_kv, "shard", axis=4, tiled=True),
    )
    all_queries = all_queries[0, 0]
    all_fresh = all_fresh[0, 0]
    step_count = all_queries.shape[1]
    model_width = all_queries.shape[2]
    local_cache = cache[0, 0, :, 0, :, :]
    cached_keys = local_cache[:, :, :key_width].reshape(row_count, slot_count, KVH, DH)
    cached_values = local_cache[:, :, key_width:].reshape(row_count, slot_count, KVH, DH)
    slot_ids = jnp.arange(slot_count, dtype=jnp.int32)
    position = jnp.where(
        section_id == 0, shard_id * slot_count + slot_ids, slot_ids * shard_count + shard_id
    )
    row_lengths = lengths[0, 0]
    visible = position[None, :] < row_lengths[:, None]
    query_heads = all_queries.reshape(row_count, step_count, KVH, group_size, DH)
    cache_scores = (
        jnp.einsum(
            "rsKgd,rcKd->rKgsc", query_heads, cached_keys, preferred_element_type=jnp.float32
        )
        * score_scale
    )
    cache_scores = jnp.where(visible[:, None, None, None, :], cache_scores, NEGATIVE)
    fresh_keys = all_fresh[:, :, :key_width].reshape(row_count, step_count, KVH, DH)
    fresh_values = all_fresh[:, :, key_width:].reshape(row_count, step_count, KVH, DH)
    fresh_scores = (
        jnp.einsum("rsKgd,rtKd->rKgst", query_heads, fresh_keys, preferred_element_type=jnp.float32)
        * score_scale
    )
    step_ids = jnp.arange(step_count, dtype=jnp.int32)
    causal = step_ids[None, :] <= step_ids[:, None]
    fresh_scores = jnp.where(causal, fresh_scores, NEGATIVE)
    cache_peak = lax.pmax(jnp.max(cache_scores, axis=-1), "shard")
    peak_score = jnp.maximum(cache_peak, jnp.max(fresh_scores, axis=-1))[..., None]
    cache_weights = jnp.exp(cache_scores - peak_score).astype(jnp.bfloat16)
    cache_mixed = jnp.einsum(
        "rKgsc,rcKd->rsKgd", cache_weights, cached_values, preferred_element_type=jnp.float32
    )
    cache_mixed = cache_mixed.reshape(row_count, step_count, model_width)
    cache_total = jnp.sum(cache_weights, axis=-1, dtype=jnp.float32)
    cache_total = jnp.transpose(cache_total, (0, 3, 1, 2)).reshape(row_count, step_count, HQ)
    own_mixed, own_total = (
        lax.psum_scatter(cache_mixed, "shard", scatter_dimension=2, tiled=True),
        lax.psum_scatter(cache_total, "shard", scatter_dimension=2, tiled=True),
    )
    fresh_weights = jnp.exp(fresh_scores - peak_score).astype(jnp.bfloat16)
    fresh_mixed = jnp.einsum(
        "rKgst,rtKd->rsKgd", fresh_weights, fresh_values, preferred_element_type=jnp.float32
    )
    fresh_mixed = fresh_mixed.reshape(row_count, step_count, model_width)
    fresh_total = jnp.sum(fresh_weights, axis=-1, dtype=jnp.float32)
    fresh_total = jnp.transpose(fresh_total, (0, 3, 1, 2)).reshape(row_count, step_count, HQ)
    head_width = model_width // shard_count
    head_count = HQ // shard_count
    fresh_mixed = lax.dynamic_slice_in_dim(fresh_mixed, shard_id * head_width, head_width, 2)
    fresh_total = lax.dynamic_slice_in_dim(fresh_total, shard_id * head_count, head_count, 2)
    combined = (own_mixed + fresh_mixed).reshape(row_count, step_count, head_count, DH)
    attended = combined / (own_total + fresh_total)[..., None]
    attended = attended.reshape(row_count, step_count, head_width).astype(jnp.bfloat16)
    destination = targets[0]
    row_ids = jnp.arange(row_count, dtype=jnp.int32)
    same_target = destination[:, None] == destination[None, :]
    target_rank = jnp.sum(same_target & (row_ids[None, :] < row_ids[:, None]), axis=1)
    out_slots = jnp.arange(group_count * CAP, dtype=jnp.int32)
    matches = (destination[None, :] == (out_slots // CAP)[:, None]) & (
        target_rank[None, :] == (out_slots % CAP)[:, None]
    )
    picker = matches.astype(jnp.bfloat16)
    picked = jnp.dot(
        picker,
        local_cache.reshape(row_count, slot_count * kv_width),
        preferred_element_type=jnp.float32,
    )
    picked = picked.astype(jnp.bfloat16).reshape(group_count * CAP, slot_count, kv_width)
    picked_fresh = jnp.einsum(
        "pr,rtw->ptw", picker, all_fresh, preferred_element_type=jnp.float32
    ).astype(jnp.bfloat16)
    picked_length = jnp.sum(jnp.where(matches, row_lengths[None, :], 0), axis=1)
    offset = position[None, :] - picked_length[:, None]
    one_hot = (offset[:, :, None] == step_ids[None, None, :]).astype(jnp.bfloat16)
    written = jnp.einsum(
        "pcs,psw->pcw", one_hot, picked_fresh, preferred_element_type=jnp.float32
    ).astype(jnp.bfloat16)
    released = jnp.where(offset[:, :, None] < 0, picked, written).reshape(
        group_count, CAP, slot_count, kv_width
    )
    carried = passed_along(released, "section", 1)
    arrived = restripe(carried)
    handed = jnp.where(section_id == 0, released, arrived)
    return (attended[None, None], handed[None, None, :, :, None, :, :])


def solution(mesh):
    in_specs = (
        P("section", "group", None, "shard", None, None),
        P("section", "group", None, None, "shard"),
        P("section", "group", None, None, "shard"),
        P("section", "group", None),
        P("group", None),
    )
    out_specs = (
        P("section", "group", None, None, "shard"),
        P("section", "group", None, None, "shard", None, None),
    )
    return jax.shard_map(
        on_device, mesh=mesh, in_specs=in_specs, out_specs=out_specs, check_vma=False
    )
```

profile of v0, /device:TPU:0, one launch (start us, length us, event | category | flops | bytes accessed | tf_op | source)
XLA Modules:
  0.0 268.7 jit_solution(329415901474090108)
XLA Ops:
  7.2 0.0 all-gather.2.cloned.1.call-start
  7.2 0.7 all-gather.2.cloned.1.call-update
  7.9 0.0 reduce-scatter.7.cloned.1.call-start
  8.0 0.7 copy.106
  8.7 32.4 %all_gather.7 = bf16[1,1,8,4,2048]{4,2,3,1,0:T(8,128)(2,1)S(1)} all-gather(bf16[1,1,8,4,256]{4,2,3,1,0:T(8,128)(2,1)S(1)} %copy.106), channel_id=1, replica_groups=mesh['section'=2,'group'=2,'shard'=8] {'shard'}, dimensions={4}, use_global_device_ids=true | all-gather | bytes 147456 | tf_op jit(solution)/shard_map/all_gather | solution.py:50
  41.1 0.9 convert_reduce_fusion.2
  42.0 0.0 copy-start.2
  42.0 6.4 %copy.142 = bf16[1,8,128,2048]{3,1,2,0:T(8,128)(2,1)} copy(bf16[1,8,128,2048]{3,2,1,0:T(8,128)(2,1)} %bitcast.111) | data formatting | bytes 8388608
  48.5 0.2 select_reduce_fusion
  48.7 0.1 broadcast_subtract_fusion
  48.8 0.2 convolution_convert_fusion.2
  48.9 0.1 broadcast_compare_fusion.1
  49.0 3.4 %convolution_convert_fusion = bf16[4,262144]{1,0:T(4,128)(2,1)S(1)} fusion(pred[4,8]{1,0:T(4,128)(4,1)S(1)} %get-tuple-element.17, bf16[8,262144]{1,0:T(8,128)(2,1)} %bitcast.110), kind=kOutput, calls=%fused_computation | convolution fusion | flops 17825792 | bytes 6291488 | tf_op jit(solution)/shard_map/dot_general | solution.py:118
  52.4 4.4 %fusion = bf16[4,128,2048]{2,1,0:T(8,128)(2,1)} fusion(bf16[1,4,128,2048]{3,1,2,0:T(4,128)(2,1)S(1)} %bitcast.118, pred[4,128]{1,0:T(4,128)(4,1)S(1)} %broadcast_compare_fusion.1, bf16[4,4,2048]{2,0,1:T(4,128)(2,1)S(1)} %convolution_convert_fusion.2, s32[4,128]{1,0:T(4,128)S(1)} %broadcast_subtract_fusion), kind=kOutput, calls=%fused_computation.2 | convolution fusion | flops 10487808 | bytes 4262400 | tf_op jit(solution)/shard_map/pcs,psw->pcw/dot_general | solution.py:130
  56.9 2.6 collective-permute-start
  59.5 6.4 %copy.102 = bf16[1,1,8,1,128,2048]{4,5,2,3,1,0:T(8,128)(2,1)} copy(bf16[1,1,8,1,128,2048]{5,4,3,2,1,0:T(8,128)(2,1)} %param.5) | data formatting | bytes 8388608 | tf_op args[0]
  66.0 0.1 broadcast_compare_fusion
  66.1 4.7 %fusion.18 = (bf16[8,128,1024]{1,2,0:T(8,128)(2,1)}, bf16[8,128,1024]{1,2,0:T(8,128)(2,1)}) fusion(bf16[8,128,2048]{1,2,0:T(8,128)(2,1)} %bitcast.112), kind=kLoop, calls=%fused_computation.51 | loop fusion | bytes 8388608 | tf_op jit(solution)/shard_map/slice | solution.py:58
  70.8 2.1 reshape.204
  72.9 2.4 bitcast_reduce_fusion
  75.3 38.5 %pmax.7 = f32[8,8,16,4]{2,3,1,0:T(4,128)S(1)} all-reduce(f32[8,8,16,4]{2,3,1,0:T(4,128)S(1)} %get-tuple-element.22), channel_id=1, replica_groups=mesh['section'=2,'group'=2,'shard'=8] {'shard'}, use_global_device_ids=true, to_apply=%region_1.2 | all-reduce | flops 4096 | bytes 32768 | tf_op jit(solution)/shard_map/pmax | solution.py:82
  113.8 3.4 %fusion.19 = (f32[8,8,16,4]{2,3,1,0:T(4,128)S(1)}, f32[8,8,16,4,4]{2,4,3,1,0:T(4,128)}) fusion(bf16[8,4,8,16,128]{4,3,2,1,0:T(8,128)(2,1)S(1)} %reshape.204, bf16[8,4,8,128,1]{3,2,0,1,4:T(8,128)(2,1)S(1)} %bitcast.125, pred[4,4]{1,0:T(4,128)(4,1)S(1)} %iota_compare_fusion.3), kind=kOutput, calls=%fused_computation.52 | convolution fusion | flops 4239360 | bytes 1196048 | tf_op jit(solution)/shard_map/rsKgd,rtKd->rKgst/dot_general | solution.py:76
  117.3 1.4 convert_reduce_fusion
  118.6 0.2 copy.138
  118.8 0.8 reshape.205
  119.6 0.0 reduce-scatter.7.cloned.1.call-update
  119.6 0.0 reduce-scatter.5.cloned.1.call-start
  119.7 2.9 %convolution_bitcast_fusion.1 = f32[8,4,8,16,128]{4,3,1,2,0:T(8,128)S(1)} fusion(bf16[8,128,8,128,1]{1,3,4,2,0:T(8,128)(2,1)} %bitcast.116, f32[8,8,128,4,16]{2,4,3,1,0:T(8,128)S(1)} %get-tuple-element.23, f32[8,8,16,4]{2,3,1,0:T(4,128)S(1)} %max.5, pred[8,128]{1,0:T(8,128)(4,1)S(1)} %broadcast_compare_fusion), kind=kOutput, calls=%fused_computation.12 | convolution fusion | flops 136314880 | bytes 6308864 | tf_op jit(solution)/shard_map/rKgsc,rcKd->rsKgd/dot_general | solution.py:85
  122.6 0.3 copy.110
  122.9 1.5 reshape.187
  124.4 0.0 reduce-scatter.5.cloned.1.call-update
  124.4 4.1 %copy.117 = bf16[2,8,2,16,2048]{4,3,2,1,0:T(8,128)(2,1)} copy(bf16[2,8,2,16,2048]{4,1,3,2,0:T(8,128)(2,1)} %bitcast.22) | data formatting | bytes 4194304 | tf_op jit(solution)/shard_map/transpose | solution.py:28
  128.5 3.9 %all-to-all-start = ((bf16[16,2,16,2048]{3,2,1,0:T(8,128)(2,1)}), bf16[16,2,16,2048]{3,2,1,0:T(8,128)(2,1)S(1)}, u32[]{:S(2)}, u32[]{:S(2)}) async-start(bf16[16,2,16,2048]{3,2,1,0:T(8,128)(2,1)} %bitcast.115), calls=%async_computation.1 | async-start | bytes 4194304 | tf_op jit(solution)/shard_map/all_to_all | solution.py:31
  132.4 0.5 convert_reduce_fusion.1
  132.9 0.1 reshape.191
  133.0 0.5 convolution_bitcast_fusion
  133.6 1.6 copy.112
  135.1 2.7 %reshape.189 = f32[8,4,16384]{2,0,1:T(8,128)} reshape(f32[8,4,8,16,128]{4,3,2,0,1:T(8,128)} %copy.112) | data formatting | bytes 4194304 | tf_op jit(solution)/shard_map/reshape | solution.py:99
  137.9 47.8 %reduce-scatter.7.cloned.1.call-done = f32[16,32]{1,0:T(8,128)} async-done(((f32[128,32]{1,0:T(8,128)}), f32[16,32]{1,0:T(8,128)}) %reduce-scatter.7.cloned.1.call-update) | async-done | bytes 2064
  185.7 0.8 reshape.206
  186.5 0.1 copy.137
  186.6 0.1 dynamic-slice_add_fusion
  186.6 0.1 copy.115
  186.7 70.2 %reduce-scatter.5.cloned.1.call-done = f32[8,4,2048]{2,0,1:T(8,128)} async-done(((f32[8,4,16384]{2,0,1:T(8,128)}), f32[8,4,2048]{2,0,1:T(8,128)}) %reduce-scatter.5.cloned.1.call-update) | async-done | bytes 262160 | tf_op jit(solution)/shard_map/reduce_scatter | solution.py:92
  256.9 1.2 fusion.9
  258.1 0.8 copy.119
  258.8 0.2 copy.118
  259.1 3.1 %select_bitcast_fusion = bf16[1,1,2,2,1,128,2048]{6,5,4,3,2,1,0:T(8,128)(2,1)} fusion(bf16[1,1,2,2,1,128,2048]{6,5,3,2,4,1,0:T(8,128)(2,1)} %bitcast.19, bf16[1,1,2,2,1,128,2048]{6,5,3,2,4,1,0:T(8,128)(2,1)S(1)} %bitcast.113, pred[]{:T(512)S(6)} %eq.30), kind=kLoop, calls=%fused_computation.8 | loop fusion | flops 1048576 | bytes 6291457
  (16 shorter events, 0.1 us)
Async XLA Ops:
  7.2 63.6 %all-gather.2.cloned.1.call-start = ((), (), s32[]{:S(2)}) async-start(), calls=%async_computation.3 | async-start | bytes 1179648 | tf_op jit(solution)/shard_map/all_gather | solution.py:49
  7.9 177.8 %reduce-scatter.7.cloned.1.call-start = ((), (), s32[]{:S(2)}) async-start(), calls=%async_computation.5 | async-start | bytes 73728
  42.0 6.5 %copy-start.1 = (s32[1,1,8]{2,1,0:T(1,128)S(1)}, s32[1,1,8]{2,1,0:T(1,128)}, u32[]{:S(2)}) copy-start(s32[1,1,8]{2,1,0:T(1,128)} %param.8) | copy-start | bytes 100
  42.0 6.5 %copy-start.2 = (s32[1,8]{1,0:T(1,128)S(1)}, s32[1,8]{1,0:T(1,128)}, u32[]{:S(2)}) copy-start(s32[1,8]{1,0:T(1,128)} %param.9) | copy-start | bytes 100
  56.9 67.5 %collective-permute-start = (bf16[2,2,128,2048]{3,2,1,0:T(8,128)(2,1)}, bf16[2,2,128,2048]{3,2,1,0:T(8,128)(2,1)}, u32[]{:S(2)}, u32[]{:S(2)}) collective-permute-start(bf16[2,2,128,2048]{3,2,1,0:T(8,128)(2,1)} %bitcast.20), channel_id=1, source_target_pairs={{0,16},{1,17},{2,18},{3,19},{4,20},{5,21},{6,22},{7,23},{8,24},{9,... | collective-permute-start | bytes 6291464 | tf_op jit(solution)/shard_map/ppermute | solution.py:20
  119.6 137.3 %reduce-scatter.5.cloned.1.call-start = ((), (), s32[]{:S(2)}) async-start(), calls=%async_computation.4 | async-start | bytes 2359296 | tf_op jit(solution)/shard_map/reduce_scatter | solution.py:92
  128.5 3.9 %copy-start = (f32[8,8,16,4,4]{2,4,3,1,0:T(4,128)S(1)}, f32[8,8,16,4,4]{2,4,3,1,0:T(4,128)}, u32[]{:S(2)}) copy-start(f32[8,8,16,4,4]{2,4,3,1,0:T(4,128)} %get-tuple-element.25) | copy-start | bytes 196612
  128.5 130.3 %all-to-all-start = ((bf16[16,2,16,2048]{3,2,1,0:T(8,128)(2,1)}), bf16[16,2,16,2048]{3,2,1,0:T(8,128)(2,1)S(1)}, u32[]{:S(2)}, u32[]{:S(2)}) async-start(bf16[16,2,16,2048]{3,2,1,0:T(8,128)(2,1)} %bitcast.115), calls=%async_computation.1 | async-start | bytes 4194304 | tf_op jit(solution)/shard_map/all_to_all | solution.py:31
Sparse Core Ops, SparseCore 0:
  10.2 42.9 all-gather.1
  119.7 65.9 reduce-scatter.6
  189.8 67.0 reduce-scatter.4
where the time goes:
time: 269 us
  waiting for transfers between devices  119 us (44%)
  blocking collectives  70.9 us (26%)
  local copies, waits for them, and re-layouts  33.7 us (13%)
  matrix products  17.3 us (6%)
  between operations  13.9 us (5%)
  other arithmetic  7.58 us (3%)
  starting transfers between devices  6.6 us (2%)
    reduce_scatter x1, waiting for transfers between devices, on_device(): lax.psum_scatter(cache_mixed, 'shard', scatter_dimension=2, tiled=True)  70.2 us
    unnamed x4, waiting for transfers between devices  48.5 us
    pmax x1, blocking collectives, on_device(): cache_peak = lax.pmax(jnp.max(cache_scores, axis=-1), 'shard')  38.5 us
    all_gather x1, blocking collectives, on_device(): lax.all_gather(fresh_kv, 'shard', axis=4, tiled=True)  32.4 us
    unnamed x17, local copies, waits for them, and re-layouts  16.2 us
  transfers between devices with their start and end apart: 5, of which 2 were waited for; matrix products, arithmetic and copies ran while one was open for 21% of the time, Pallas kernels for 0%

commit v1 on v0

v1 whole, which is shorter than its diff:
```python
import functools
import math

import jax
import jax.numpy as jnp
from jax import lax
from jax.experimental import pallas as pl
from jax.experimental.pallas import tpu as pltpu
from jax.sharding import PartitionSpec as P

HQ = 128
KVH = 8
DH = 128
CAP = 2
FAR = -1e30
MESH = pl.DeviceIdType.MESH
F32 = jnp.float32
BF16 = jnp.bfloat16


def kernel(
    dims,
    cache_ref,
    q_ref,
    fresh_ref,
    len_ref,
    tgt_ref,
    att_ref,
    handed_ref,
    cv,
    fg,
    ff,
    qg,
    part,
    got,
    stat,
    gstat,
    fac,
    rel,
    perm,
    load_sem,
    out_sem,
    fs,
    fr,
    qs,
    qr,
    ps,
    pr,
    ss,
    sr,
    hs,
    hr,
):
    n, groups, rows, steps, slots, width = dims
    me = lax.axis_index("shard")
    sec = lax.axis_index("section")
    grp = lax.axis_index("group")
    hc = HQ // n
    sg = steps * hc
    wb = width // n
    pp = slots // n
    scale = 1.0 / math.sqrt(DH)
    other = 1 - sec

    load = pltpu.make_async_copy(cache_ref, cv, load_sem)
    load.start()

    barrier = pltpu.get_barrier_semaphore()

    def greet_peer(i, c):
        pl.semaphore_signal(
            barrier, inc=1, device_id={"shard": lax.rem(me + i, n)}, device_id_type=MESH
        )
        return c

    def greet_other(i, c):
        pl.semaphore_signal(
            barrier,
            inc=1,
            device_id={"section": other, "group": i // n, "shard": i % n},
            device_id_type=MESH,
        )
        return c

    lax.fori_loop(1, n, greet_peer, 0)
    lax.fori_loop(0, groups * n, greet_other, 0)
    pl.semaphore_wait(barrier, n - 1 + groups * n)

    def fresh_copy(to, slot):
        return pltpu.make_async_remote_copy(
            fresh_ref, fg.at[slot], fs.at[to], fr.at[slot], {"shard": to}, MESH
        )

    def query_copy(to, slot):
        return pltpu.make_async_remote_copy(
            q_ref, qg.at[slot], qs.at[to], qr.at[slot], {"shard": to}, MESH
        )

    def part_copy(to, slot):
        return pltpu.make_async_remote_copy(
            part.at[to], got.at[slot], ps.at[to], pr.at[slot], {"shard": to}, MESH
        )

    def stat_copy(to, slot):
        return pltpu.make_async_remote_copy(
            stat.at[to], gstat.at[slot], ss.at[to], sr.at[slot], {"shard": to}, MESH
        )

    def hand_copy(grp_to, shard_to, slot_grp, slot_shard):
        return pltpu.make_async_remote_copy(
            perm.at[grp_to, shard_to],
            handed_ref.at[slot_grp, :, slot_shard],
            hs.at[grp_to * n + shard_to],
            hr.at[slot_grp * n + slot_shard],
            {"section": 1, "group": grp_to, "shard": shard_to},
            MESH,
        )

    def send_fresh(i, c):
        fresh_copy(lax.rem(me + i, n), me).start()
        return c

    def send_query(i, c):
        query_copy(lax.rem(me + i, n), me).start()
        return c

    lax.fori_loop(1, n, send_fresh, 0)
    lax.fori_loop(1, n, send_query, 0)

    fg[me] = fresh_ref[...]
    qg[me] = q_ref[...]

    def wait_fresh(i, c):
        fresh_copy(me, lax.rem(me + n - i, n)).wait_recv()
        return c

    lax.fori_loop(1, n, wait_fresh, 0)
    per = max(1, 128 // wb)
    for j in range(0, n, per):
        pieces = [fg[j + i].astype(F32) for i in range(per)]
        piece = pieces[0] if per == 1 else jnp.concatenate(pieces, axis=1)
        for r in range(rows):
            ff[r, :, j * wb : (j + per) * wb] = piece[r * steps : (r + 1) * steps]
    load.wait()

    slot_rows = lax.broadcasted_iota(jnp.int32, (slots, 128), 0)
    place_rows = jnp.where(sec == 0, me * slots + slot_rows, slot_rows * n + me)

    def insert(r, c):
        off = place_rows - len_ref[r]
        keep = (off < 0).astype(F32).astype(BF16)
        hot = [(off == t).astype(F32).astype(BF16) for t in range(steps)]
        lines = ff[r]
        for w in range(width // 128):
            cols = slice(w * 128, (w + 1) * 128)
            y = cv[r, :, cols] * keep
            for t in range(steps):
                line = jnp.broadcast_to(lines[t : t + 1, cols], (slots, 128)).astype(BF16)
                y = y + hot[t] * line
            cv[r, :, cols] = y
        return c

    lax.fori_loop(0, rows, insert, 0)

    @pl.when(sec == 0)
    def _():
        q_ids = lax.broadcasted_iota(jnp.int32, (slots, slots), 0)
        i_ids = lax.broadcasted_iota(jnp.int32, (slots, slots), 1)
        order = ((q_ids % pp) * n + q_ids // pp == i_ids).astype(F32)
        tgt = [tgt_ref[r] for r in range(rows)]
        tile = 512
        for d in range(groups):
            count = jnp.int32(0)
            src = [jnp.int32(0)] * CAP
            for r in range(rows):
                hit = tgt[r] == d
                for k in range(CAP):
                    src[k] = jnp.where(hit & (count == k), r, src[k])
                count = count + hit.astype(jnp.int32)
            for k in range(CAP):
                live = (count > k).astype(F32)
                mover = (order * live).astype(BF16)
                for w in range(0, width, tile):
                    x = cv[src[k], :, w : w + tile]
                    y = (x.astype(F32) * live).reshape(n, pp, tile).astype(BF16)
                    rel[d, k, :, :, w : w + tile] = y
                    z = jnp.dot(mover, x, preferred_element_type=F32)
                    perm[d, :, k, :, w : w + tile] = z.reshape(n, pp, tile).astype(BF16)
        pltpu.make_async_copy(rel, handed_ref, out_sem).start()

        def send_hand(i, c):
            to = lax.rem(me + i, n)
            for d in range(groups):
                dst_group = lax.rem(grp + d, groups)
                hand_copy(dst_group, to, grp, me).start()
            return c

        lax.fori_loop(0, n, send_hand, 0)

    lane = lax.broadcasted_iota(jnp.int32, (sg, slots), 1)
    sub = lax.broadcasted_iota(jnp.int32, (sg, slots), 0)
    place = jnp.where(sec == 0, me * slots + lane, lane * n + me) - sub // hc
    stat_lane = lax.broadcasted_iota(jnp.int32, (sg, 128), 1)

    def attend(i, c):
        j = lax.rem(me + n - i, n)

        @pl.when(i > 0)
        def _():
            query_copy(me, j).wait_recv()

        kv = (j * hc) // (HQ // KVH)
        k_cols = pl.ds(pl.multiple_of(kv * DH, DH), DH)
        v_cols = pl.ds(pl.multiple_of((KVH + kv) * DH, DH), DH)
        lse_all = jnp.zeros((sg, 128), F32)
        for r in range(rows):
            s = lax.dot_general(
                qg[j, r],
                cv[r, :, k_cols],
                (((1,), (1,)), ((), ())),
                preferred_element_type=F32,
            )
            s = jnp.where(place <= len_ref[r], s * scale, FAR)
            m = jnp.max(s, axis=1, keepdims=True)
            p = jnp.exp(s - m).astype(BF16)
            total = jnp.sum(p.astype(F32), axis=1, keepdims=True)
            o = jnp.dot(p, cv[r, :, v_cols], preferred_element_type=F32)
            part[j, r] = (o / total).astype(BF16)
            lse_all = jnp.where(stat_lane == r, m + jnp.log(total), lse_all)
        stat[j] = lse_all

        @pl.when(i > 0)
        def _():
            stat_copy(j, me).start()
            part_copy(j, me).start()

        return c

    lax.fori_loop(0, n, attend, 0)
    gstat[me] = stat[me]
    got[me] = part[me]

    def wait_stat(i, c):
        stat_copy(me, lax.rem(me + i, n)).wait_recv()
        return c

    lax.fori_loop(1, n, wait_stat, 0)
    peak = gstat[0]
    for j in range(1, n):
        peak = jnp.maximum(peak, gstat[j])
    total = jnp.zeros_like(peak)
    for j in range(n):
        e = jnp.exp(gstat[j] - peak)
        fac[j] = e
        total = total + e
    inverse = 1.0 / total

    def wait_part(i, c):
        part_copy(me, lax.rem(me + i, n)).wait_recv()
        return c

    lax.fori_loop(1, n, wait_part, 0)
    for r in range(rows):
        acc = jnp.zeros((sg, DH), F32)
        for j in range(n):
            acc = acc + got[j, r].astype(F32) * fac[j, :, r : r + 1]
        att_ref[r] = (acc * inverse[:, r : r + 1]).astype(BF16)

    def wait_sends(i, c):
        to = lax.rem(me + i, n)
        fresh_copy(to, me).wait_send()
        query_copy(to, me).wait_send()
        stat_copy(to, me).wait_send()
        part_copy(to, me).wait_send()
        return c

    lax.fori_loop(1, n, wait_sends, 0)

    @pl.when(sec == 0)
    def _():
        def wait_hand(i, c):
            hand_copy(i // n, i % n, grp, me).wait_send()
            return c

        lax.fori_loop(0, groups * n, wait_hand, 0)
        pltpu.make_async_copy(rel, handed_ref, out_sem).wait()

    @pl.when(sec == 1)
    def _():
        def wait_hand(i, c):
            hand_copy(grp, me, i // n, i % n).wait_recv()
            return c

        lax.fori_loop(0, groups * n, wait_hand, 0)


def on_device(n, groups, cache, queries, fresh_kv, lengths, targets):
    rows, slots, width = cache.shape[2], cache.shape[4], cache.shape[5]
    steps = queries.shape[3]
    hc = HQ // n
    sg = steps * hc
    wb = width // n
    pp = slots // n
    dims = (n, groups, rows, steps, slots, width)
    vmem = pl.BlockSpec(memory_space=pltpu.VMEM)
    smem = pl.BlockSpec(memory_space=pltpu.SMEM)
    hbm = pl.BlockSpec(memory_space=pl.ANY)
    dma = pltpu.SemaphoreType.DMA
    attended, handed = pl.pallas_call(
        functools.partial(kernel, dims),
        out_shape=(
            jax.ShapeDtypeStruct((rows, sg, DH), BF16),
            jax.ShapeDtypeStruct((groups, CAP, n, pp, width), BF16),
        ),
        in_specs=[hbm, vmem, vmem, smem, smem],
        out_specs=(vmem, hbm),
        scratch_shapes=[
            pltpu.VMEM((rows, slots, width), BF16),
            pltpu.VMEM((n, rows * steps, wb), BF16),
            pltpu.VMEM((rows, steps, width), F32),
            pltpu.VMEM((n, rows, sg, DH), BF16),
            pltpu.VMEM((n, rows, sg, DH), BF16),
            pltpu.VMEM((n, rows, sg, DH), BF16),
            pltpu.VMEM((n, sg, 128), F32),
            pltpu.VMEM((n, sg, 128), F32),
            pltpu.VMEM((n, sg, 128), F32),
            pltpu.VMEM((groups, CAP, n, pp, width), BF16),
            pltpu.VMEM((groups, n, CAP, pp, width), BF16),
            dma,
            dma,
            dma((n,)),
            dma((n,)),
            dma((n,)),
            dma((n,)),
            dma((n,)),
            dma((n,)),
            dma((n,)),
            dma((n,)),
            dma((groups * n,)),
            dma((groups * n,)),
        ],
        compiler_params=pltpu.CompilerParams(
            collective_id=0, has_side_effects=True, vmem_limit_bytes=56 * 1024 * 1024
        ),
    )(
        cache.reshape(rows, slots, width),
        queries.reshape(rows, sg, DH),
        fresh_kv.reshape(rows * steps, wb),
        lengths.reshape(rows),
        targets.reshape(rows),
    )
    return (
        attended.reshape(1, 1, rows, steps, hc * DH),
        handed.reshape(1, 1, groups, CAP, 1, slots, width),
    )


def solution(mesh):
    in_specs = (
        P("section", "group", None, "shard", None, None),
        P("section", "group", None, None, "shard"),
        P("section", "group", None, None, "shard"),
        P("section", "group", None),
        P("group", None),
    )
    out_specs = (
        P("section", "group", None, None, "shard"),
        P("section", "group", None, None, "shard", None, None),
    )
    return jax.shard_map(
        functools.partial(on_device, mesh.shape["shard"], mesh.shape["group"]),
        mesh=mesh,
        in_specs=in_specs,
        out_specs=out_specs,
        check_vma=False,
    )
```

time: 269 us -> 97 us (0.36)
  waiting for transfers between devices: 119 us -> 0 us
  Pallas kernels: 0 us -> 88.4 us
  blocking collectives: 70.9 us -> 0 us
  local copies, waits for them, and re-layouts: 33.7 us -> 7.73 us
  matrix products: 17.3 us -> 0 us
  between operations: 13.9 us -> 0.64 us
  other arithmetic: 7.58 us -> 0 us
  starting transfers between devices: 6.6 us -> 0 us
    pallas_call x0 -> x1, Pallas kernels: none -> 88.4 us  [on_device(): pl.pallas_call(functools.partial(kernel, dims), out_shape=(jax.ShapeDtype...]
    reduce_scatter x1 -> x0, waiting for transfers between devices: 70.2 us -> none  [on_device(): lax.psum_scatter(cache_mixed, 'shard', scatter_dimension=2, tiled=True)]
    unnamed x4 -> x0, waiting for transfers between devices: 48.5 us -> none
    pmax x1 -> x0, blocking collectives: 38.5 us -> none  [on_device(): cache_peak = lax.pmax(jnp.max(cache_scores, axis=-1), 'shard')]
    all_gather x1 -> x0, blocking collectives: 32.4 us -> none  [on_device(): lax.all_gather(fresh_kv, 'shard', axis=4, tiled=True)]
    dot_general x7 -> x0, matrix products: 17.3 us -> none  [the longest x1 4.45 us: on_device(): jnp.einsum('pcs,psw->pcw', one_hot, picked_fresh, preferred_element_type=...]
    unnamed x17 -> x1, local copies, waits for them, and re-layouts: 16.2 us -> 3.16 us
    transpose x5 -> x0, local copies, waits for them, and re-layouts: 6.2 us -> none  [the longest x1 4.1 us: restripe(): jnp.transpose(pieces, (0, 3, 1, 2, 4))]
  transfers between devices with their start and end apart: 5 -> 0, of which waited for: 2 -> 0; matrix products, arithmetic and copies ran while one was open for 21% -> 0% of each run, Pallas kernels for 0% -> 0%
where the time goes in v1:
time: 97 us; the launch traced here: 96.8 us
  Pallas kernels  88.4 us (91%)
  local copies, waits for them, and re-layouts  7.73 us (8%)
    pallas_call x1, Pallas kernels, on_device(): pl.pallas_call(functools.partial(kernel, dims), out_shape=(jax.ShapeDtype...  88.4 us
    unnamed x1, local copies, waits for them, and re-layouts  3.16 us

profile of v1, /device:TPU:0, one launch (start us, length us, event | category | flops | bytes accessed | tf_op | source)
XLA Modules:
  0.0 96.8 jit_solution(18382381813289822334)
XLA Ops:
  0.6 1.3 %reshape.27.fresh_ref = bf16[32,256]{1,0:T(8,128)(2,1)} reshape(bf16[1,1,8,4,256]{4,3,2,1,0:T(4,128)(2,1)} %param.7) | data formatting | bytes 32768 | tf_op jit(solution)/shard_map/reshape | solution.py:348
  2.0 1.6 %reshape.26.q_ref = bf16[8,64,128]{2,1,0:T(8,128)(2,1)} reshape(bf16[1,1,8,4,2048]{4,3,2,1,0:T(4,128)(2,1)} %param.6) | data formatting | bytes 262144 | tf_op jit(solution)/shard_map/reshape | solution.py:347
  3.6 88.4 %shard_map.68 = (bf16[8,64,128]{2,1,0:T(8,128)(2,1)}, bf16[2,2,8,16,2048]{4,3,2,1,0:T(8,128)(2,1)}) custom-call(bf16[8,128,2048]{2,1,0:T(8,128)(2,1)} %bitcast.6, bf16[8,64,128]{2,1,0:T(8,128)(2,1)} %reshape.26.q_ref, bf16[32,256]{1,0:T(8,128)(2,1)} %reshape.27.fresh_ref, s32[8]{0:T(128)} %bitcast.8, s32[8]{0:T(128)} %bitcast.9), custom_call_target="tpu_custom_call" | custom-call | tf_op jit(solution)/shard_map/pallas_call | solution.py:309
  92.0 1.6 %reshape.30 = bf16[1,1,8,4,2048]{4,3,2,1,0:T(4,128)(2,1)} reshape(bf16[8,64,128]{2,1,0:T(8,128)(2,1)} %get-tuple-element.4) | data formatting | bytes 262144 | tf_op jit(solution)/shard_map/reshape | solution.py:353
  93.6 3.2 %copy.9 = bf16[1,1,2,2,1,128,2048]{6,5,4,3,2,1,0:T(8,128)(2,1)} copy(bf16[1,1,2,2,1,128,2048]{6,5,4,3,2,1,0:T(8,128)(2,1)} %bitcast.7) | data formatting | bytes 4194304

commit v2 on v1

v2 whole, which is shorter than its diff:
```python
import functools
import math

import jax
import jax.numpy as jnp
from jax import lax
from jax.experimental import pallas as pl
from jax.experimental.pallas import tpu as pltpu
from jax.sharding import PartitionSpec as P

HQ = 128
KVH = 8
DH = 128
CAP = 2
FAR = -1e30
MESH = pl.DeviceIdType.MESH
F32 = jnp.float32
BF16 = jnp.bfloat16


def kernel(
    dims,
    cache_ref,
    q_ref,
    fresh_ref,
    len_ref,
    tgt_ref,
    att_ref,
    handed_ref,
    cv,
    fg,
    ff,
    qg,
    part,
    got,
    stat,
    gstat,
    part2,
    got2,
    stat2,
    gstat2,
    rel,
    perm,
    load_sem,
    out_sem,
    fs,
    fr,
    qs,
    qdown,
    qx,
    qr,
    ps,
    pr,
    ss,
    sr,
    ps2,
    pr2,
    ss2,
    sr2,
    hs,
    hr,
):
    n, groups, rows, steps, slots, width = dims
    nx = side(n)
    nz = n // nx
    me = lax.axis_index("shard")
    sec = lax.axis_index("section")
    grp = lax.axis_index("group")
    z = me // nx
    x = lax.rem(me, nx)
    hc = HQ // n
    sg = steps * hc
    wb = width // n
    pp = slots // n
    scale = 1.0 / math.sqrt(DH)
    other = 1 - sec

    load = pltpu.make_async_copy(cache_ref, cv, load_sem)
    load.start()

    barrier = pltpu.get_barrier_semaphore()

    def greet_peer(i, c):
        pl.semaphore_signal(
            barrier, inc=1, device_id={"shard": lax.rem(me + i, n)}, device_id_type=MESH
        )
        return c

    def greet_other(i, c):
        pl.semaphore_signal(
            barrier,
            inc=1,
            device_id={"section": other, "group": i // n, "shard": i % n},
            device_id_type=MESH,
        )
        return c

    lax.fori_loop(1, n, greet_peer, 0)
    lax.fori_loop(0, groups * n, greet_other, 0)

    for r in range(rows):
        line = q_ref[r].astype(F32)
        qg[me, r] = jnp.concatenate(
            [line[:, g * DH : (g + 1) * DH] for g in range(hc)], axis=0
        ).astype(BF16)

    pl.semaphore_wait(barrier, n - 1 + groups * n)

    def fresh_copy(to, slot):
        return pltpu.make_async_remote_copy(
            fresh_ref, fg.at[slot], fs.at[to], fr.at[slot], {"shard": to}, MESH
        )

    def query_copy(slot, to, sem):
        return pltpu.make_async_remote_copy(
            qg.at[slot], qg.at[slot], sem, qr.at[slot], {"shard": to}, MESH
        )

    def across(i):
        return z * nx + lax.rem(x + i, nx)

    def part_copy(to_x, block, src_x):
        return pltpu.make_async_remote_copy(
            part.at[to_x * nz + block],
            got.at[src_x * nz + block],
            ps.at[to_x * nz + block],
            pr.at[src_x * nz + block],
            {"shard": z * nx + to_x},
            MESH,
        )

    def stat_copy(to_x, block, src_x):
        return pltpu.make_async_remote_copy(
            stat.at[to_x * nz + block],
            gstat.at[src_x * nz + block],
            ss.at[to_x * nz + block],
            sr.at[src_x * nz + block],
            {"shard": z * nx + to_x},
            MESH,
        )

    def part2_copy(to_z, src_z):
        return pltpu.make_async_remote_copy(
            part2.at[to_z],
            got2.at[src_z],
            ps2.at[to_z],
            pr2.at[src_z],
            {"shard": to_z * nx + x},
            MESH,
        )

    def stat2_copy(to_z, src_z):
        return pltpu.make_async_remote_copy(
            stat2.at[to_z],
            gstat2.at[src_z],
            ss2.at[to_z],
            sr2.at[src_z],
            {"shard": to_z * nx + x},
            MESH,
        )

    def hand_copy(grp_to, shard_to, slot_grp, slot_shard):
        return pltpu.make_async_remote_copy(
            perm.at[grp_to, shard_to],
            handed_ref.at[slot_grp, :, slot_shard],
            hs.at[grp_to * n + shard_to],
            hr.at[slot_grp * n + slot_shard],
            {"section": 1, "group": grp_to, "shard": shard_to},
            MESH,
        )

    def send_fresh(i, c):
        fresh_copy(lax.rem(me + i, n), me).start()
        return c

    lax.fori_loop(1, n, send_fresh, 0)

    def up(slot):
        return query_copy(slot, me + nx, qs.at[slot])

    def down(slot):
        return query_copy(slot, me - nx, qs.at[slot])

    def own_down():
        return query_copy(me, me - nx, qdown)

    def sideways(slot, i):
        return query_copy(slot, across(i), qx.at[(slot // nx) * nx + i])

    @pl.when(z < nz - 1)
    def _():
        up(me).start()

    @pl.when(z > 0)
    def _():
        own_down().start()

    for i in range(1, nx):
        sideways(me, i).start()

    def pass_on(d):
        low = me - d * nx
        high = me + d * nx

        @pl.when(z >= d)
        def _():
            query_copy(low, me, qr.at[low]).wait_recv()
            for i in range(1, nx):
                sideways(low, i).start()

            @pl.when(z < nz - 1)
            def _():
                up(low).start()

        @pl.when(z + d < nz)
        def _():
            query_copy(high, me, qr.at[high]).wait_recv()
            for i in range(1, nx):
                sideways(high, i).start()

            @pl.when(z > 0)
            def _():
                down(high).start()

    fg[me] = fresh_ref[...]

    def wait_fresh(i, c):
        fresh_copy(me, lax.rem(me + n - i, n)).wait_recv()
        return c

    lax.fori_loop(1, n, wait_fresh, 0)
    pass_on(1)
    per = max(1, 128 // wb)
    for j in range(0, n, per):
        pieces = [fg[j + i].astype(F32) for i in range(per)]
        ff[:, :, j * wb : (j + per) * wb] = (
            pieces[0] if per == 1 else jnp.concatenate(pieces, axis=2)
        )
    load.wait()

    slot_rows = lax.broadcasted_iota(jnp.int32, (slots, 128), 0)
    place_rows = jnp.where(sec == 0, me * slots + slot_rows, slot_rows * n + me)

    def insert(r, c):
        off = place_rows - len_ref[r]
        keep = (off < 0).astype(F32).astype(BF16)
        hot = [(off == t).astype(F32).astype(BF16) for t in range(steps)]
        lines = ff[r]
        for w in range(width // 128):
            cols = slice(w * 128, (w + 1) * 128)
            y = cv[r, :, cols] * keep
            for t in range(steps):
                line = jnp.broadcast_to(lines[t : t + 1, cols], (slots, 128)).astype(BF16)
                y = y + hot[t] * line
            cv[r, :, cols] = y
        return c

    lax.fori_loop(0, rows, insert, 0)
    if nz > 2:
        pass_on(2)

    @pl.when(sec == 0)
    def _():
        q_ids = lax.broadcasted_iota(jnp.int32, (slots, slots), 0)
        i_ids = lax.broadcasted_iota(jnp.int32, (slots, slots), 1)
        order = ((q_ids % pp) * n + q_ids // pp == i_ids).astype(F32)
        tgt = [tgt_ref[r] for r in range(rows)]
        tile = 512
        for d in range(groups):
            count = jnp.int32(0)
            src = [jnp.int32(0)] * CAP
            for r in range(rows):
                hit = tgt[r] == d
                for k in range(CAP):
                    src[k] = jnp.where(hit & (count == k), r, src[k])
                count = count + hit.astype(jnp.int32)
            for k in range(CAP):
                live = (count > k).astype(F32)
                mover = (order * live).astype(BF16)
                for w in range(0, width, tile):
                    y = cv[src[k], :, w : w + tile]
                    v = (y.astype(F32) * live).reshape(n, pp, tile).astype(BF16)
                    rel[d, k, :, :, w : w + tile] = v
                    v = jnp.dot(mover, y, preferred_element_type=F32)
                    perm[d, :, k, :, w : w + tile] = v.reshape(n, pp, tile).astype(BF16)
        pltpu.make_async_copy(rel, handed_ref, out_sem).start()

        def send_hand(i, c):
            to = lax.rem(me + i, n)
            for d in range(groups):
                hand_copy(lax.rem(grp + d, groups), to, grp, me).start()
            return c

        lax.fori_loop(0, n, send_hand, 0)

    for d in range(3, nz):
        pass_on(d)

    lane = lax.broadcasted_iota(jnp.int32, (sg, slots), 1)
    sub = lax.broadcasted_iota(jnp.int32, (sg, slots), 0)
    place = jnp.where(sec == 0, me * slots + lane, lane * n + me) - sub % steps
    stat_lane = lax.broadcasted_iota(jnp.int32, (sg, 128), 1)
    ones = jnp.ones((slots, DH), BF16)
    batch = 4

    def attend(j, row_list):
        kv = (j * hc) // (HQ // KVH)
        k_cols = pl.ds(pl.multiple_of(kv * DH, DH), DH)
        v_cols = pl.ds(pl.multiple_of((KVH + kv) * DH, DH), DH)
        scores = [
            lax.dot_general(
                qg[j, r],
                cv[r, :, k_cols],
                (((1,), (1,)), ((), ())),
                preferred_element_type=F32,
            )
            for r in row_list
        ]
        scores = [
            jnp.where(place <= len_ref[r], s * scale, FAR) for r, s in zip(row_list, scores)
        ]
        peaks = [jnp.max(s, axis=1, keepdims=True) for s in scores]
        weights = [jnp.exp(s - m).astype(BF16) for s, m in zip(scores, peaks)]
        mixed = [
            jnp.dot(
                p,
                jnp.concatenate([cv[r, :, v_cols], ones], axis=1),
                preferred_element_type=F32,
            )
            for r, p in zip(row_list, weights)
        ]
        out = []
        for m, o in zip(peaks, mixed):
            total = o[:, DH:]
            out.append((o[:, :DH] / total, m + jnp.log(total)))
        return out

    def first(i, c):
        to_x = lax.rem(x + 1 + i // nz, nx)
        block = lax.rem(z + i, nz)
        j = block * nx + to_x
        query_copy(j, me, qr.at[j]).wait_recv()
        slot = to_x * nz + block
        lse_all = jnp.zeros((sg, 128), F32)
        for r0 in range(0, rows, batch):
            row_list = list(range(r0, r0 + batch))
            for r, (o, lse) in zip(row_list, attend(j, row_list)):
                part[slot, r] = o.astype(BF16)
                lse_all = jnp.where(stat_lane == r, lse, lse_all)
        stat[slot] = jnp.transpose(lse_all)[:rows]
        stat_copy(to_x, block, x).start()
        part_copy(to_x, block, x).start()
        return c

    lax.fori_loop(0, (nx - 1) * nz, first, 0)

    def second(i, c):
        block = lax.rem(z + 1 + i, nz)
        j = block * nx + x
        for k in range(1, nx):
            src_x = lax.rem(x + k, nx)
            stat_copy(src_x, block, src_x).wait_recv()
            part_copy(src_x, block, src_x).wait_recv()
        theirs = [
            jnp.transpose(gstat[lax.rem(x + k, nx) * nz + block]) for k in range(1, nx)
        ]
        lse_all = jnp.zeros((sg, 128), F32)
        for r0 in range(0, rows, batch):
            row_list = list(range(r0, r0 + batch))
            for r, (o, lse) in zip(row_list, attend(j, row_list)):
                far = [jnp.broadcast_to(t[:, r : r + 1], (sg, DH)) for t in theirs]
                peak = functools.reduce(jnp.maximum, far, lse)
                e = jnp.exp(lse - peak)
                acc = o * e
                total = e
                for k in range(1, nx):
                    e = jnp.exp(far[k - 1] - peak)
                    slot = lax.rem(x + k, nx) * nz + block
                    acc = acc + got[slot, r].astype(F32) * e
                    total = total + e
                part2[block, r] = (acc / total).astype(BF16)
                lse_all = jnp.where(stat_lane == r, peak + jnp.log(total), lse_all)
        stat2[block] = jnp.transpose(lse_all)[:rows]

        @pl.when(i < nz - 1)
        def _():
            stat2_copy(block, z).start()
            part2_copy(block, z).start()

        return c

    lax.fori_loop(0, nz, second, 0)
    gstat2[z] = stat2[z]
    got2[z] = part2[z]

    def wait_stat(i, c):
        from_z = lax.rem(z + i, nz)
        stat2_copy(from_z, from_z).wait_recv()
        return c

    lax.fori_loop(1, nz, wait_stat, 0)
    peak = functools.reduce(jnp.maximum, [gstat2[j] for j in range(nz)])
    es = [jnp.exp(gstat2[j] - peak) for j in range(nz)]
    inverse = 1.0 / sum(es[1:], es[0])
    fac = [jnp.transpose(e * inverse) for e in es]

    def wait_part(i, c):
        from_z = lax.rem(z + i, nz)
        part2_copy(from_z, from_z).wait_recv()
        return c

    lax.fori_loop(1, nz, wait_part, 0)
    for r in range(rows):
        acc = jnp.zeros((sg, DH), F32)
        for j in range(nz):
            acc = acc + got2[j, r].astype(F32) * fac[j][:, r : r + 1]
        for g in range(hc):
            att_ref[r, :, g * DH : (g + 1) * DH] = acc[g * steps : (g + 1) * steps].astype(BF16)

    def wait_fresh_sends(i, c):
        fresh_copy(lax.rem(me + i, n), me).wait_send()
        return c

    lax.fori_loop(1, n, wait_fresh_sends, 0)

    @pl.when(z < nz - 1)
    def _():
        up(me).wait_send()

    @pl.when(z > 0)
    def _():
        own_down().wait_send()

    def wait_queries(block, c):
        slot = block * nx + x
        for i in range(1, nx):
            sideways(slot, i).wait_send()

        @pl.when((block < z) & (z < nz - 1))
        def _():
            up(slot).wait_send()

        @pl.when((block > z) & (z > 0))
        def _():
            down(slot).wait_send()

        return c

    lax.fori_loop(0, nz, wait_queries, 0)

    def wait_parts(i, c):
        to_x = lax.rem(x + 1 + i // nz, nx)
        stat_copy(to_x, lax.rem(z + i, nz), x).wait_send()
        part_copy(to_x, lax.rem(z + i, nz), x).wait_send()
        return c

    lax.fori_loop(0, (nx - 1) * nz, wait_parts, 0)

    def wait_parts2(i, c):
        stat2_copy(lax.rem(z + i, nz), z).wait_send()
        part2_copy(lax.rem(z + i, nz), z).wait_send()
        return c

    lax.fori_loop(1, nz, wait_parts2, 0)

    @pl.when(sec == 0)
    def _():
        def wait_hand(i, c):
            hand_copy(i // n, i % n, grp, me).wait_send()
            return c

        lax.fori_loop(0, groups * n, wait_hand, 0)
        pltpu.make_async_copy(rel, handed_ref, out_sem).wait()

    @pl.when(sec == 1)
    def _():
        def wait_hand(i, c):
            hand_copy(grp, me, i // n, i % n).wait_recv()
            return c

        lax.fori_loop(0, groups * n, wait_hand, 0)


def side(n):
    nx = max(1, math.isqrt(n // 2))
    while n % nx:
        nx -= 1
    return nx


def on_device(n, groups, cache, queries, fresh_kv, lengths, targets):
    rows, slots, width = cache.shape[2], cache.shape[4], cache.shape[5]
    steps = queries.shape[3]
    hc = HQ // n
    sg = steps * hc
    wb = width // n
    pp = slots // n
    nz = n // side(n)
    dims = (n, groups, rows, steps, slots, width)
    vmem = pl.BlockSpec(memory_space=pltpu.VMEM)
    smem = pl.BlockSpec(memory_space=pltpu.SMEM)
    hbm = pl.BlockSpec(memory_space=pl.ANY)
    dma = pltpu.SemaphoreType.DMA
    attended, handed = pl.pallas_call(
        functools.partial(kernel, dims),
        out_shape=(
            jax.ShapeDtypeStruct((rows, steps, hc * DH), BF16),
            jax.ShapeDtypeStruct((groups, CAP, n, pp, width), BF16),
        ),
        in_specs=[hbm, vmem, vmem, smem, smem],
        out_specs=(vmem, hbm),
        scratch_shapes=[
            pltpu.VMEM((rows, slots, width), BF16),
            pltpu.VMEM((n, rows, steps, wb), BF16),
            pltpu.VMEM((rows, steps, width), F32),
            pltpu.VMEM((n, rows, sg, DH), BF16),
            pltpu.VMEM((n, rows, sg, DH), BF16),
            pltpu.VMEM((n, rows, sg, DH), BF16),
            pltpu.VMEM((n, rows, sg), F32),
            pltpu.VMEM((n, rows, sg), F32),
            pltpu.VMEM((nz, rows, sg, DH), BF16),
            pltpu.VMEM((nz, rows, sg, DH), BF16),
            pltpu.VMEM((nz, rows, sg), F32),
            pltpu.VMEM((nz, rows, sg), F32),
            pltpu.VMEM((groups, CAP, n, pp, width), BF16),
            pltpu.VMEM((groups, n, CAP, pp, width), BF16),
            dma,
            dma,
            dma((n,)),
            dma((n,)),
            dma((n,)),
            dma,
            dma((n,)),
            dma((n,)),
            dma((n,)),
            dma((n,)),
            dma((n,)),
            dma((n,)),
            dma((nz,)),
            dma((nz,)),
            dma((nz,)),
            dma((nz,)),
            dma((groups * n,)),
            dma((groups * n,)),
        ],
        compiler_params=pltpu.CompilerParams(
            collective_id=0, has_side_effects=True, vmem_limit_bytes=56 * 1024 * 1024
        ),
    )(
        cache.reshape(rows, slots, width),
        queries.reshape(rows, steps, hc * DH),
        fresh_kv.reshape(rows, steps, wb),
        lengths.reshape(rows),
        targets.reshape(rows),
    )
    return (
        attended.reshape(1, 1, rows, steps, hc * DH),
        handed.reshape(1, 1, groups, CAP, 1, slots, width),
    )


def solution(mesh):
    in_specs = (
        P("section", "group", None, "shard", None, None),
        P("section", "group", None, None, "shard"),
        P("section", "group", None, None, "shard"),
        P("section", "group", None),
        P("group", None),
    )
    out_specs = (
        P("section", "group", None, None, "shard"),
        P("section", "group", None, None, "shard", None, None),
    )
    return jax.shard_map(
        functools.partial(on_device, mesh.shape["shard"], mesh.shape["group"]),
        mesh=mesh,
        in_specs=in_specs,
        out_specs=out_specs,
        check_vma=False,
    )
```

time: 97 us -> 65.3 us (0.67)
  Pallas kernels: 88.4 us -> 59.7 us
  local copies, waits for them, and re-layouts: 7.73 us -> 4.76 us
    pallas_call x1, Pallas kernels: 88.4 us -> 59.7 us  [on_device(): pl.pallas_call(functools.partial(kernel, dims), out_shape=(jax.ShapeDtype...]
    reshape x3 -> x0, local copies, waits for them, and re-layouts: 4.57 us -> none  [the longest x1 1.64 us: on_device(): queries.reshape(rows, sg, DH)]
    unnamed x1 -> x2, local copies, waits for them, and re-layouts: 3.16 us -> 4.76 us
where the time goes in v2:
time: 65.3 us; the launch traced here: 65.2 us
  Pallas kernels  59.7 us (91%)
  local copies, waits for them, and re-layouts  4.76 us (7%)
    pallas_call x1, Pallas kernels, on_device(): pl.pallas_call(functools.partial(kernel, dims), out_shape=(jax.ShapeDtype...  59.7 us
    unnamed x2, local copies, waits for them, and re-layouts  4.76 us

profile of v2, /device:TPU:0, one launch (start us, length us, event | category | flops | bytes accessed | tf_op | source)
XLA Modules:
  0.0 65.2 jit_solution(10348207940769434667)
XLA Ops:
  0.6 59.7 %shard_map.68 = (bf16[8,4,2048]{2,1,0:T(4,128)(2,1)}, bf16[2,2,8,16,2048]{4,3,2,1,0:T(8,128)(2,1)}) custom-call(bf16[8,128,2048]{2,1,0:T(8,128)(2,1)} %bitcast.9, bf16[8,4,2048]{2,1,0:T(4,128)(2,1)} %bitcast.11, bf16[8,4,256]{2,1,0:T(4,128)(2,1)} %bitcast.13, s32[8]{0:T(128)} %bitcast.14, s32[8]{0:T(128)} %bitcast.15), custom_call_target="tpu_custom_call" | custom-call | tf_op jit(solution)/shard_map/pallas_call | solution.py:504
  60.4 1.6 %copy.10 = bf16[1,1,8,4,2048]{4,3,2,1,0:T(4,128)(2,1)} copy(bf16[1,1,8,4,2048]{4,3,2,1,0:T(4,128)(2,1)} %bitcast.12) | data formatting | bytes 262144
  62.0 3.2 %copy.11 = bf16[1,1,2,2,1,128,2048]{6,5,4,3,2,1,0:T(8,128)(2,1)} copy(bf16[1,1,2,2,1,128,2048]{6,5,4,3,2,1,0:T(8,128)(2,1)} %bitcast.10) | data formatting | bytes 4194304

commit v3 on v2

--- a/solution.py
+++ b/solution.py
@@ -238,6 +238,44 @@
         )
     load.wait()
 
+    def pick(d):
+        count = jnp.int32(0)
+        src = [jnp.int32(0)] * CAP
+        for r in range(rows):
+            hit = tgt_ref[r] == d
+            for k in range(CAP):
+                src[k] = jnp.where(hit & (count == k), r, src[k])
+            count = count + hit.astype(jnp.int32)
+        return src, [count > k for k in range(CAP)]
+
+    @pl.when(sec == 0)
+    def _():
+        q_ids = lax.broadcasted_iota(jnp.int32, (slots, slots), 0)
+        i_ids = lax.broadcasted_iota(jnp.int32, (slots, slots), 1)
+        order = (q_ids % pp) * n + q_ids // pp == i_ids
+        tile = 512
+        ids = lax.broadcasted_iota(jnp.int32, (slots, tile), 0)
+        at = me * slots + (ids % pp) * n + ids // pp
+        for d in range(groups):
+            src, lives = pick(d)
+            for k in range(CAP):
+                size = jnp.where(lives[k], len_ref[src[k]], -steps)
+                mover = (order & (me * slots + i_ids < size)).astype(F32).astype(BF16)
+                hot = [(at == size + t).astype(F32) for t in range(steps)]
+                lines = ff[src[k]]
+                for w in range(0, width, tile):
+                    v = jnp.dot(mover, cv[src[k], :, w : w + tile], preferred_element_type=F32)
+                    for t in range(steps):
+                        v = v + hot[t] * lines[t : t + 1, w : w + tile]
+                    perm[d, :, k, :, w : w + tile] = v.reshape(n, pp, tile).astype(BF16)
+
+            def send_hand(i, c):
+                hand_copy(d, lax.rem(me + i, n), grp, me).start()
+                return c
+
+            lax.fori_loop(0, n, send_hand, 0)
+
+
     slot_rows = lax.broadcasted_iota(jnp.int32, (slots, 128), 0)
     place_rows = jnp.where(sec == 0, me * slots + slot_rows, slot_rows * n + me)
 
@@ -256,45 +294,19 @@
         return c
 
     lax.fori_loop(0, rows, insert, 0)
-    if nz > 2:
-        pass_on(2)
-
+    for d in range(2, nz):
+        pass_on(d)
     @pl.when(sec == 0)
     def _():
-        q_ids = lax.broadcasted_iota(jnp.int32, (slots, slots), 0)
-        i_ids = lax.broadcasted_iota(jnp.int32, (slots, slots), 1)
-        order = ((q_ids % pp) * n + q_ids // pp == i_ids).astype(F32)
-        tgt = [tgt_ref[r] for r in range(rows)]
         tile = 512
         for d in range(groups):
-            count = jnp.int32(0)
-            src = [jnp.int32(0)] * CAP
-            for r in range(rows):
-                hit = tgt[r] == d
-                for k in range(CAP):
-                    src[k] = jnp.where(hit & (count == k), r, src[k])
-                count = count + hit.astype(jnp.int32)
+            src, lives = pick(d)
             for k in range(CAP):
-                live = (count > k).astype(F32)
-                mover = (order * live).astype(BF16)
+                live = lives[k].astype(F32)
                 for w in range(0, width, tile):
-                    y = cv[src[k], :, w : w + tile]
-                    v = (y.astype(F32) * live).reshape(n, pp, tile).astype(BF16)
-                    rel[d, k, :, :, w : w + tile] = v
-                    v = jnp.dot(mover, y, preferred_element_type=F32)
-                    perm[d, :, k, :, w : w + tile] = v.reshape(n, pp, tile).astype(BF16)
+                    y = cv[src[k], :, w : w + tile].astype(F32) * live
+                    rel[d, k, :, :, w : w + tile] = y.reshape(n, pp, tile).astype(BF16)
         pltpu.make_async_copy(rel, handed_ref, out_sem).start()
-
-        def send_hand(i, c):
-            to = lax.rem(me + i, n)
-            for d in range(groups):
-                hand_copy(lax.rem(grp + d, groups), to, grp, me).start()
-            return c
-
-        lax.fori_loop(0, n, send_hand, 0)
-
-    for d in range(3, nz):
-        pass_on(d)
 
     lane = lax.broadcasted_iota(jnp.int32, (sg, slots), 1)
     sub = lax.broadcasted_iota(jnp.int32, (sg, slots), 0)
@@ -335,9 +347,17 @@
             out.append((o[:, :DH] / total, m + jnp.log(total)))
         return out
 
-    def first(i, c):
-        to_x = lax.rem(x + 1 + i // nz, nx)
-        block = lax.rem(z + i, nz)
+    below = z
+    above = nz - 1 - z
+
+    def near(i):
+        step = (i + 1) // 2
+        inner = jnp.where(lax.rem(i, 2) == 1, z + step, z - step)
+        outer = jnp.where(above > below, i, nz - 1 - i)
+        return jnp.where(i <= 2 * jnp.minimum(below, above), inner, outer)
+
+    def first(block, k, c):
+        to_x = lax.rem(x + k, nx)
         j = block * nx + to_x
         query_copy(j, me, qr.at[j]).wait_recv()
         slot = to_x * nz + block
@@ -352,10 +372,7 @@
         part_copy(to_x, block, x).start()
         return c
 
-    lax.fori_loop(0, (nx - 1) * nz, first, 0)
-
-    def second(i, c):
-        block = lax.rem(z + 1 + i, nz)
+    def second(block):
         j = block * nx + x
         for k in range(1, nx):
             src_x = lax.rem(x + k, nx)
@@ -382,14 +399,32 @@
                 lse_all = jnp.where(stat_lane == r, peak + jnp.log(total), lse_all)
         stat2[block] = jnp.transpose(lse_all)[:rows]
 
-        @pl.when(i < nz - 1)
+        @pl.when(block != z)
         def _():
             stat2_copy(block, z).start()
             part2_copy(block, z).start()
 
-        return c
-
-    lax.fori_loop(0, nz, second, 0)
+    def turn(t, c):
+        @pl.when(t < nz)
+        def _():
+            lax.fori_loop(1, nx, functools.partial(first, near(t)), 0)
+
+        @pl.when(t >= 2)
+        def _():
+            second(jnp.where(t <= nz, near(t - 1), z))
+
+        return c
+
+    def turn_a(t, c):
+        lax.fori_loop(1, nx, functools.partial(first, lax.rem(z + t, nz)), 0)
+        return c
+
+    def turn_b(t, c):
+        second(lax.rem(z + 1 + t, nz))
+        return c
+
+    lax.fori_loop(0, nz, turn_a, 0)
+    lax.fori_loop(0, nz, turn_b, 0)
     gstat2[z] = stat2[z]
     got2[z] = part2[z]
 

time: 65.3 us -> 64.1 us (0.982)
  Pallas kernels: 59.7 us -> 58.5 us
    pallas_call x1, Pallas kernels: 59.7 us -> 58.5 us  [on_device(): pl.pallas_call(functools.partial(kernel, dims), out_shape=(jax.ShapeDtype...]
where the time goes in v3:
time: 64.1 us; the launch traced here: 63.9 us
  Pallas kernels  58.5 us (91%)
  local copies, waits for them, and re-layouts  4.76 us (7%)
    pallas_call x1, Pallas kernels, on_device(): pl.pallas_call(functools.partial(kernel, dims), out_shape=(jax.ShapeDtype...  58.5 us
    unnamed x2, local copies, waits for them, and re-layouts  4.76 us

profile of v3, /device:TPU:0, one launch (start us, length us, event | category | flops | bytes accessed | tf_op | source)
XLA Modules:
  0.0 63.9 jit_solution(1958698741946501762)
XLA Ops:
  0.6 58.5 %shard_map.68 = (bf16[8,4,2048]{2,1,0:T(4,128)(2,1)}, bf16[2,2,8,16,2048]{4,3,2,1,0:T(8,128)(2,1)}) custom-call(bf16[8,128,2048]{2,1,0:T(8,128)(2,1)} %bitcast.9, bf16[8,4,2048]{2,1,0:T(4,128)(2,1)} %bitcast.11, bf16[8,4,256]{2,1,0:T(4,128)(2,1)} %bitcast.13, s32[8]{0:T(128)} %bitcast.14, s32[8]{0:T(128)} %bitcast.15), custom_call_target="tpu_custom_call" | custom-call | tf_op jit(solution)/shard_map/pallas_call | solution.py:539
  59.1 1.6 %copy.10 = bf16[1,1,8,4,2048]{4,3,2,1,0:T(4,128)(2,1)} copy(bf16[1,1,8,4,2048]{4,3,2,1,0:T(4,128)(2,1)} %bitcast.12) | data formatting | bytes 262144
  60.7 3.2 %copy.11 = bf16[1,1,2,2,1,128,2048]{6,5,4,3,2,1,0:T(8,128)(2,1)} copy(bf16[1,1,2,2,1,128,2048]{6,5,4,3,2,1,0:T(8,128)(2,1)} %bitcast.10) | data formatting | bytes 4194304
